TPU v7x, 512 devices: a whole 4x8x8 slice. The times are simulated.
512 devices in a mesh: segment: 4 (over z_lo), expert: 128 (over z_hi, y, x, core).
Axes of the slice: x: 4, y: 8, z: 8 (z_hi: 2, z_lo: 4; z = z_hi * 4 + z_lo), core: 2. Of those that a mesh axis runs over, the one named last changes fastest.
Arguments:
- forward_input: bfloat16 [4, 1024, 2048], P('segment', 'expert'), may hold values from -6 to 6
- forward_routes: int32 [4, 1024, 6], P('segment', 'expert'), may hold values from 0 to 31, all different within a row; in each aligned block of 8 rows (0 to 7, 8 to 15, ..., all dimensions but the last counted through in order) at most 2 rows name the same one
- forward_gates: float32 [4, 1024, 6], P('segment', 'expert'), may hold values from 0.1 to 1
- backward_grad: bfloat16 [4, 1024, 2048], P('segment', 'expert'), may hold values from -6 to 6
- backward_routes: int32 [4, 1024, 6], P('segment', 'expert'), may hold values from 0 to 31, all different within a row; in each aligned block of 8 rows (0 to 7, 8 to 15, ..., all dimensions but the last counted through in order) at most 2 rows name the same one
- backward_gates: float32 [4, 1024, 6], P('segment', 'expert'), may hold values from 0.1 to 1
- saved_gate_up: bfloat16 [4, 1024, 6, 2, 1024], P('segment', 'expert'), may hold values from -6 to 6
- w_gate_up: bfloat16 [4, 2048, 2, 32768], P('segment', None, None, 'expert'), may hold values from -0.125 to 0.125
- w_down: bfloat16 [4, 32768, 2048], P('segment', 'expert'), may hold values from -0.1875 to 0.1875
Outputs:
- forward_output: bfloat16 [4, 1024, 2048], P('segment', 'expert')
- input_grad: bfloat16 [4, 1024, 2048], P('segment', 'expert')
Inputs may be any that keep to these rules, and one draw needn't show every extreme that they name: `forward_routes`: each row names 6 different experts. Among the 8 rows of one device no expert is named more than 2 times; some device names some expert exactly 2 times, and loads differ from expert to expert. `backward_routes`: each row names 6 different experts. Among the 8 rows of one device no expert is named more than 2 times; some device names some expert exactly 2 times, and loads differ from expert to expert.
All inputs are finite; a program needn't handle non-finite values.
Results may differ from a plain program's by a relative error of at most 0.007.
Values may be sent and summed in bfloat16 or wider, within the bound.
A program may use at most 64 MiB of HBM per device.

v0:
```python
import jax
import jax.numpy as jnp
from jax import lax
from jax.sharding import PartitionSpec as P

EXPERTS = 32
TOP = 6
CAP = 2


def shifted(block, axis, distance):
    devices = range(lax.axis_size(axis))
    route = [((i - distance) % len(devices), i) for i in devices]
    return lax.ppermute(block, axis, route)


def route_slots(routes, capacity, split_count, local_experts):
    token_count, fanout = routes.shape
    flat_routes = routes.reshape(token_count * fanout)
    expert_grid = lax.broadcasted_iota(jnp.int32, (token_count * fanout, EXPERTS), 1)
    onehot = (flat_routes[:, None] == expert_grid).astype(jnp.int32)
    route_ranks = jnp.sum(jnp.cumsum(onehot, axis=0) * onehot, axis=1) - 1
    group_base = flat_routes // local_experts * (split_count * local_experts * capacity)
    slot_base = group_base + flat_routes % local_experts * capacity + route_ranks
    offsets = lax.broadcasted_iota(jnp.int32, (1, split_count), 1) * (local_experts * capacity)
    return slot_base[:, None] + offsets


def slot_matrix(positions, slot_count):
    slot_ids = lax.broadcasted_iota(jnp.int32, (slot_count, 1, 1), 0)
    return jnp.sum((positions[None, :, :] == slot_ids).astype(jnp.int32), axis=2)


def expert_forward(received, weights_pair, weights_down):
    source_count, local_experts, items, row_width = received.shape
    part_width = weights_down.shape[0] // local_experts
    flat_rows = jnp.transpose(received, (1, 0, 2, 3)).reshape(
        local_experts, source_count * items, row_width
    )
    pair_parts = weights_pair.reshape(row_width, 2, local_experts, part_width)
    both_values = jnp.einsum(
        "erd,dgef->egrf", flat_rows, pair_parts, preferred_element_type=jnp.float32
    )
    hidden = (jax.nn.silu(both_values[:, 0]) * both_values[:, 1]).astype(jnp.bfloat16)
    down_parts = weights_down.reshape(local_experts, part_width, row_width)
    result = jnp.einsum(
        "erf,efd->erd", hidden, down_parts, preferred_element_type=jnp.float32
    ).astype(jnp.bfloat16)
    return jnp.transpose(
        result.reshape(local_experts, source_count, items, row_width), (1, 0, 2, 3)
    )


def expert_backward(grads_in, pairs_in, weights_pair, weights_down):
    source_count, local_experts, items, row_width = grads_in.shape
    part_width = weights_down.shape[0] // local_experts
    flat_grads = jnp.transpose(grads_in, (1, 0, 2, 3)).reshape(
        local_experts, source_count * items, row_width
    )
    flat_pairs = jnp.transpose(pairs_in, (1, 0, 2, 3, 4)).reshape(
        local_experts, source_count * items, 2, part_width
    )
    down_parts = weights_down.reshape(local_experts, part_width, row_width)
    grad_hidden = jnp.einsum(
        "erd,efd->erf", flat_grads, down_parts, preferred_element_type=jnp.float32
    )
    gate_value = flat_pairs[:, :, 0].astype(jnp.float32)
    upper_value = flat_pairs[:, :, 1].astype(jnp.float32)
    sigmoid_gate = jax.nn.sigmoid(gate_value)
    grad_gate = (
        grad_hidden * upper_value * sigmoid_gate * (1.0 + gate_value * (1.0 - sigmoid_gate))
    ).astype(jnp.bfloat16)
    grad_upper = (grad_hidden * jax.nn.silu(gate_value)).astype(jnp.bfloat16)
    stacked = jnp.stack([grad_gate, grad_upper], axis=1)
    pair_parts = weights_pair.reshape(row_width, 2, local_experts, part_width)
    grad_rows = jnp.einsum(
        "egrf,dgef->erd", stacked, pair_parts, preferred_element_type=jnp.float32
    ).astype(jnp.bfloat16)
    return jnp.transpose(
        grad_rows.reshape(local_experts, source_count, items, row_width), (1, 0, 2, 3)
    )


def combine_routes(partial_value, positions, route_gates):
    token_count, fanout = route_gates.shape
    row_width = partial_value.shape[-1]
    returned = lax.all_to_all(partial_value, "expert", split_axis=0, concat_axis=0, tiled=True)
    flat_back = returned.reshape(-1, row_width)
    per_route = jnp.sum(flat_back[positions].astype(jnp.float32), axis=1)
    weighted = per_route.reshape(token_count, fanout, row_width) * route_gates[:, :, None]
    return jnp.sum(weighted, axis=1)


def on_device(
    forward_input,
    forward_routes,
    forward_gates,
    backward_grad,
    backward_routes,
    backward_gates,
    saved_gate_up,
    w_gate_up,
    w_down,
):
    device_count = lax.axis_size("expert")
    split_count = max(1, device_count // EXPERTS)
    local_experts = max(1, EXPERTS // device_count)
    capacity = CAP
    slot_count = device_count * local_experts * capacity
    weights_pair = w_gate_up[0]
    weights_down = w_down[0]
    part_width = weights_down.shape[0] // local_experts
    arrived = shifted(forward_input, "segment", 1)[0]
    returning = shifted(backward_grad, "segment", -1)[0]
    token_count, row_width = arrived.shape
    forward_slots = route_slots(forward_routes[0], capacity, split_count, local_experts)
    forward_match = slot_matrix(forward_slots, slot_count)
    token_match = jnp.sum(forward_match.reshape(slot_count, token_count, TOP), axis=2).astype(
        jnp.bfloat16
    )
    outgoing = jnp.dot(token_match, arrived, preferred_element_type=jnp.float32).astype(
        jnp.bfloat16
    )
    outgoing = outgoing.reshape(device_count, local_experts, capacity, row_width)
    forward_partial = expert_forward(
        lax.all_to_all(outgoing, "expert", split_axis=0, concat_axis=0, tiled=True),
        weights_pair,
        weights_down,
    )
    forward_mix = combine_routes(forward_partial, forward_slots, forward_gates[0])
    forward_output = (arrived.astype(jnp.float32) + forward_mix).astype(jnp.bfloat16)
    backward_slots = route_slots(backward_routes[0], capacity, split_count, local_experts)
    backward_match = slot_matrix(backward_slots, slot_count)
    route_count = token_count * TOP
    grad_match = jnp.sum(backward_match.reshape(slot_count, token_count, TOP), axis=2).astype(
        jnp.bfloat16
    )
    grad_outgoing = jnp.dot(grad_match, returning, preferred_element_type=jnp.float32).astype(
        jnp.bfloat16
    )
    grad_outgoing = grad_outgoing.reshape(device_count, local_experts, capacity, row_width)
    group_count = device_count // split_count
    route_weights = backward_match.astype(jnp.bfloat16).reshape(
        group_count, split_count, local_experts * capacity, route_count
    )
    route_weights = jnp.transpose(route_weights, (1, 0, 2, 3)).reshape(
        split_count, group_count * local_experts * capacity, route_count
    )
    saved_parts = saved_gate_up[0].reshape(route_count, 2, split_count, part_width)
    saved_parts = jnp.transpose(saved_parts, (2, 0, 1, 3)).reshape(
        split_count, route_count, 2 * part_width
    )
    picked = jnp.einsum(
        "jpr,jrf->jpf", route_weights, saved_parts, preferred_element_type=jnp.float32
    ).astype(jnp.bfloat16)
    picked = picked.reshape(split_count, group_count, local_experts, capacity, 2, part_width)
    pair_outgoing = jnp.transpose(picked, (1, 0, 2, 3, 4, 5)).reshape(
        device_count, local_experts, capacity, 2, part_width
    )
    backward_partial = expert_backward(
        lax.all_to_all(grad_outgoing, "expert", split_axis=0, concat_axis=0, tiled=True),
        lax.all_to_all(pair_outgoing, "expert", split_axis=0, concat_axis=0, tiled=True),
        weights_pair,
        weights_down,
    )
    backward_mix = combine_routes(backward_partial, backward_slots, backward_gates[0])
    input_grad = (returning.astype(jnp.float32) + backward_mix).astype(jnp.bfloat16)
    return (forward_output[None], input_grad[None])


def solution(mesh):
    placed = (
        P("segment", "expert", None),
        P("segment", "expert", None),
        P("segment", "expert", None),
        P("segment", "expert", None),
        P("segment", "expert", None),
        P("segment", "expert", None),
        P("segment", "expert", None, None, None),
        P("segment", None, None, "expert"),
        P("segment", "expert", None),
    )
    return jax.shard_map(
        on_device,
        mesh=mesh,
        in_specs=placed,
        out_specs=(P("segment", "expert", None), P("segment", "expert", None)),
        check_vma=False,
    )
```

profile of v0, /device:TPU:1, one launch (start us, length us, event | category | flops | bytes accessed | tf_op | source)
XLA Modules:
  0.0 224.9 jit_solution(425549842440056097)
XLA Ops:
  6.5 20.8 %all-to-all-start.3 = ((bf16[128,1,2,2,256]{4,2,3,1,0:T(2,128)(2,1)}), bf16[128,1,2,2,256]{4,2,3,1,0:T(2,128)(2,1)S(1)}, u32[]{:S(2)}, u32[]{:S(2)}) async-start(bf16[128,1,2,2,256]{4,2,3,1,0:T(2,128)(2,1)} %bitcast.20), calls=%async_computation.3 | async-start | bytes 524288 | tf_op jit(solution)/shard_map/all_to_all | solution.py:162
  27.4 4.9 %collective-permute-start.1 = (bf16[1,8,2048]{2,1,0:T(8,128)(2,1)S(1)}, bf16[1,8,2048]{2,1,0:T(8,128)(2,1)S(1)}, u32[]{:S(2)}, u32[]{:S(2)}) collective-permute-start(bf16[1,8,2048]{2,1,0:T(8,128)(2,1)S(1)} %copy-done.14), channel_id=1, source_target_pairs={{128,0},{256,128},{384,256},{0,384},{129,1},{257,129},{385,257},{1... | collective-permute-start | bytes 98312 | tf_op jit(solution)/shard_map/ppermute | solution.py:14
  35.3 11.1 %all-to-all-done.3 = bf16[128,1,2,2,256]{4,2,3,1,0:T(2,128)(2,1)S(1)} async-done(((bf16[128,1,2,2,256]{4,2,3,1,0:T(2,128)(2,1)}), bf16[128,1,2,2,256]{4,2,3,1,0:T(2,128)(2,1)S(1)}, u32[]{:S(2)}, u32[]{:S(2)}) %all-to-all-start.3) | async-done | bytes 262176 | tf_op jit(solution)/shard_map/all_to_all | solution.py:162
  46.4 7.5 %all-to-all-start.2 = ((bf16[128,1,2,2048]{3,2,1,0:T(2,128)(2,1)}), bf16[128,1,2,2048]{3,2,1,0:T(2,128)(2,1)S(1)}, u32[]{:S(2)}, u32[]{:S(2)}) async-start(bf16[128,1,2,2048]{3,2,1,0:T(2,128)(2,1)} %bitcast.86), calls=%async_computation.2 | async-start | bytes 2097152 | tf_op jit(solution)/shard_map/all_to_all | solution.py:161
  53.9 1.9 collective-permute-start
  55.9 14.5 %collective-permute-done = bf16[1,8,2048]{2,1,0:T(8,128)(2,1)S(1)} collective-permute-done((bf16[1,8,2048]{2,1,0:T(8,128)(2,1)}, bf16[1,8,2048]{2,1,0:T(8,128)(2,1)S(1)}, u32[]{:S(2)}, u32[]{:S(2)}) %collective-permute-start) | collective-permute-done | bytes 32800 | tf_op jit(solution)/shard_map/ppermute | solution.py:14
  71.8 2.5 %reshape.308 = bf16[128,1,2,2048]{3,2,0,1:T(2,128)(2,1)} reshape(bf16[256,2048]{1,0:T(8,128)(2,1)} %convolution_convert_fusion.1) | data formatting | bytes 2097152 | tf_op jit(solution)/shard_map/reshape | solution.py:124
  74.4 15.1 %all-to-all-done.2 = bf16[128,1,2,2048]{3,2,1,0:T(2,128)(2,1)S(1)} async-done(((bf16[128,1,2,2048]{3,2,1,0:T(2,128)(2,1)}), bf16[128,1,2,2048]{3,2,1,0:T(2,128)(2,1)S(1)}, u32[]{:S(2)}, u32[]{:S(2)}) %all-to-all-start.2) | async-done | bytes 1048608 | tf_op jit(solution)/shard_map/all_to_all | solution.py:161
  89.5 6.9 %all-to-all-start = ((bf16[128,1,2,2048]{3,2,1,0:T(2,128)(2,1)}), bf16[128,1,2,2048]{3,2,1,0:T(2,128)(2,1)}, u32[]{:S(2)}, u32[]{:S(2)}) async-start(bf16[128,1,2,2048]{3,2,1,0:T(2,128)(2,1)} %bitcast.87), calls=%async_computation | async-start | bytes 2097152 | tf_op jit(solution)/shard_map/all_to_all | solution.py:126
  99.6 2.0 fusion.25
  103.9 27.7 %all-to-all-done = bf16[128,1,2,2048]{3,2,1,0:T(2,128)(2,1)} async-done(((bf16[128,1,2,2048]{3,2,1,0:T(2,128)(2,1)}), bf16[128,1,2,2048]{3,2,1,0:T(2,128)(2,1)}, u32[]{:S(2)}, u32[]{:S(2)}) %all-to-all-start) | async-done | bytes 1048608 | tf_op jit(solution)/shard_map/all_to_all | solution.py:126
  131.6 5.5 %all-to-all-start.4 = ((bf16[128,1,2,2048]{3,2,1,0:T(2,128)(2,1)}), bf16[128,1,2,2048]{3,2,1,0:T(2,128)(2,1)S(1)}, u32[]{:S(2)}, u32[]{:S(2)}) async-start(bf16[128,1,2,2048]{3,2,1,0:T(2,128)(2,1)} %bitcast.88), calls=%async_computation.4 | async-start | bytes 2097152 | tf_op jit(solution)/shard_map/all_to_all | solution.py:87
  137.1 2.3 %reshape.346 = bf16[256,2048,1]{1,0,2:T(8,128)(2,1)} reshape(bf16[128,1,2,2048]{3,2,1,0:T(2,128)(2,1)} %all-to-all-done) | data formatting | bytes 2097152 | tf_op jit(solution)/shard_map/reshape.1
  139.4 2.0 fusion.4
  142.9 2.6 %transpose_reshape.6 = bf16[128,1,2,2048]{3,2,0,1:T(2,128)(2,1)} reshape(bf16[256,2048]{1,0:T(8,128)(2,1)} %convolution_convert_fusion.2) | data formatting | bytes 2097152 | tf_op jit(solution)/shard_map/transpose;reshape | solution.py:49
  145.4 26.6 %all-to-all-done.4 = bf16[128,1,2,2048]{3,2,1,0:T(2,128)(2,1)S(1)} async-done(((bf16[128,1,2,2048]{3,2,1,0:T(2,128)(2,1)}), bf16[128,1,2,2048]{3,2,1,0:T(2,128)(2,1)S(1)}, u32[]{:S(2)}, u32[]{:S(2)}) %all-to-all-start.4) | async-done | bytes 1048608 | tf_op jit(solution)/shard_map/all_to_all | solution.py:87
  172.1 6.4 %all-to-all-start.1 = ((bf16[128,1,2,2048]{3,2,1,0:T(2,128)(2,1)}), bf16[128,1,2,2048]{3,2,1,0:T(2,128)(2,1)}, u32[]{:S(2)}, u32[]{:S(2)}) async-start(bf16[128,1,2,2048]{3,2,1,0:T(2,128)(2,1)} %bitcast.85), calls=%async_computation.1 | async-start | bytes 2097152 | tf_op jit(solution)/shard_map/all_to_all | solution.py:87
  180.5 2.0 gather_fusion.1
  182.5 2.6 %reshape.345 = f32[48,4,2048]{2,1,0:T(4,128)} reshape(bf16[192,2048]{1,0:T(8,128)(2,1)} %gather_fusion.1) | data formatting | bytes 2359296 | tf_op jit(solution)/shard_map/convert_element_type | solution.py:89
  185.1 2.4 %reduce_sum.103 = f32[48,2048]{1,0:T(8,128)S(1)} reduce(f32[48,4,2048]{2,1,0:T(4,128)} %reshape.345, f32[]{:T(128)} %constant.62.clone.1), dimensions={1}, to_apply=%region_10.11 | reduce | flops 294912 | bytes 1966084 | tf_op jit(solution)/shard_map/reduce_sum | solution.py:89
  188.4 24.6 %all-to-all-done.1 = bf16[128,1,2,2048]{3,2,1,0:T(2,128)(2,1)} async-done(((bf16[128,1,2,2048]{3,2,1,0:T(2,128)(2,1)}), bf16[128,1,2,2048]{3,2,1,0:T(2,128)(2,1)}, u32[]{:S(2)}, u32[]{:S(2)}) %all-to-all-start.1) | async-done | bytes 1048608 | tf_op jit(solution)/shard_map/all_to_all | solution.py:87
  214.5 2.0 gather_fusion
  216.5 2.7 %reshape.344 = f32[48,4,2048]{2,1,0:T(4,128)} reshape(bf16[192,2048]{1,0:T(8,128)(2,1)} %gather_fusion) | data formatting | bytes 2359296 | tf_op jit(solution)/shard_map/convert_element_type | solution.py:89
  219.2 2.4 %reduce_sum.97 = f32[48,2048]{1,0:T(8,128)S(1)} reduce(f32[48,4,2048]{2,1,0:T(4,128)} %reshape.344, f32[]{:T(128)} %constant.62.clone.1), dimensions={1}, to_apply=%region_4.5 | reduce | flops 294912 | bytes 1966084 | tf_op jit(solution)/shard_map/reduce_sum | solution.py:89
  (83 shorter events, 24.7 us)
Async XLA Ops:
  0.6 101.0 %copy-start = (bf16[1,2048,2,256]{3,2,1,0:T(2,128)(2,1)S(1)}, bf16[1,2048,2,256]{3,2,1,0:T(2,128)(2,1)}, u32[]{:S(2)}) copy-start(bf16[1,2048,2,256]{3,2,1,0:T(2,128)(2,1)} %param.16) | copy-start | bytes 6291460
  0.6 26.7 %copy-start.14 = (bf16[1,8,2048]{2,1,0:T(8,128)(2,1)S(1)}, bf16[1,8,2048]{2,1,0:T(8,128)(2,1)}, u32[]{:S(2)}) copy-start(bf16[1,8,2048]{2,1,0:T(8,128)(2,1)} %param.12) | copy-start | bytes 98308
  0.7 2.7 %copy-start.7 = (s32[4]{0:T(128)}, s32[4]{0:T(128)S(1)}, u32[]{:S(2)}) copy-start(s32[4]{0:T(128)S(1)} %iota_multiply_fusion) | copy-start | bytes 52
  2.9 0.6 copy-start.9
  3.2 0.6 copy-start.11
  6.5 39.9 %all-to-all-start.3 = ((bf16[128,1,2,2,256]{4,2,3,1,0:T(2,128)(2,1)}), bf16[128,1,2,2,256]{4,2,3,1,0:T(2,128)(2,1)S(1)}, u32[]{:S(2)}, u32[]{:S(2)}) async-start(bf16[128,1,2,2,256]{4,2,3,1,0:T(2,128)(2,1)} %bitcast.20), calls=%async_computation.3 | async-start | bytes 524288 | tf_op jit(solution)/shard_map/all_to_all | solution.py:162
  27.4 5.9 %collective-permute-start.1 = (bf16[1,8,2048]{2,1,0:T(8,128)(2,1)S(1)}, bf16[1,8,2048]{2,1,0:T(8,128)(2,1)S(1)}, u32[]{:S(2)}, u32[]{:S(2)}) collective-permute-start(bf16[1,8,2048]{2,1,0:T(8,128)(2,1)S(1)} %copy-done.14), channel_id=1, source_target_pairs={{128,0},{256,128},{384,256},{0,384},{129,1},{257,129},{385,257},{1... | collective-permute-start | bytes 98312 | tf_op jit(solution)/shard_map/ppermute | solution.py:14
  33.3 13.1 %copy-start.3 = (bf16[1,8,2048]{2,1,0:T(8,128)(2,1)}, bf16[1,8,2048]{2,1,0:T(8,128)(2,1)S(1)}, u32[]{:S(2)}) copy-start(bf16[1,8,2048]{2,1,0:T(8,128)(2,1)S(1)} %collective-permute-done.1) | copy-start | bytes 98308
  46.4 43.1 %all-to-all-start.2 = ((bf16[128,1,2,2048]{3,2,1,0:T(2,128)(2,1)}), bf16[128,1,2,2048]{3,2,1,0:T(2,128)(2,1)S(1)}, u32[]{:S(2)}, u32[]{:S(2)}) async-start(bf16[128,1,2,2048]{3,2,1,0:T(2,128)(2,1)} %bitcast.86), calls=%async_computation.2 | async-start | bytes 2097152 | tf_op jit(solution)/shard_map/all_to_all | solution.py:161
  53.9 16.4 %collective-permute-start = (bf16[1,8,2048]{2,1,0:T(8,128)(2,1)}, bf16[1,8,2048]{2,1,0:T(8,128)(2,1)S(1)}, u32[]{:S(2)}, u32[]{:S(2)}) collective-permute-start(bf16[1,8,2048]{2,1,0:T(8,128)(2,1)} %param.9), channel_id=1, source_target_pairs={{384,0},{0,128},{128,256},{256,384},{385,1},{1,129},{129,257},{257... | collective-permute-start | bytes 98312 | tf_op jit(solution)/shard_map/ppermute | solution.py:14
  70.4 19.1 %copy-start.4 = (bf16[1,8,2048]{2,1,0:T(8,128)(2,1)}, bf16[1,8,2048]{2,1,0:T(8,128)(2,1)S(1)}, u32[]{:S(2)}) copy-start(bf16[1,8,2048]{2,1,0:T(8,128)(2,1)S(1)} %collective-permute-done) | copy-start | bytes 98308
  89.5 42.1 %all-to-all-start = ((bf16[128,1,2,2048]{3,2,1,0:T(2,128)(2,1)}), bf16[128,1,2,2048]{3,2,1,0:T(2,128)(2,1)}, u32[]{:S(2)}, u32[]{:S(2)}) async-start(bf16[128,1,2,2048]{3,2,1,0:T(2,128)(2,1)} %bitcast.87), calls=%async_computation | async-start | bytes 2097152 | tf_op jit(solution)/shard_map/all_to_all | solution.py:126
  131.6 40.4 %all-to-all-start.4 = ((bf16[128,1,2,2048]{3,2,1,0:T(2,128)(2,1)}), bf16[128,1,2,2048]{3,2,1,0:T(2,128)(2,1)S(1)}, u32[]{:S(2)}, u32[]{:S(2)}) async-start(bf16[128,1,2,2048]{3,2,1,0:T(2,128)(2,1)} %bitcast.88), calls=%async_computation.4 | async-start | bytes 2097152 | tf_op jit(solution)/shard_map/all_to_all | solution.py:87
  139.4 2.0 copy-start.13
  142.9 35.6 %copy-start.5 = (f32[1,8,6]{1,0,2:T(1,128)S(1)}, f32[1,8,6]{1,0,2:T(1,128)}, u32[]{:S(2)}) copy-start(f32[1,8,6]{1,0,2:T(1,128)} %param.11) | copy-start | bytes 580
  142.9 35.7 %copy-start.6 = (f32[1,8,6]{1,0,2:T(1,128)S(1)}, f32[1,8,6]{1,0,2:T(1,128)}, u32[]{:S(2)}) copy-start(f32[1,8,6]{1,0,2:T(1,128)} %param.14) | copy-start | bytes 580
  142.9 35.8 %copy-start.8 = (s32[4]{0:T(128)S(1)}, s32[4]{0:T(128)}, u32[]{:S(2)}) copy-start(s32[4]{0:T(128)} %copy-done.7) | copy-start | bytes 52
  142.9 35.8 %copy-start.10 = (s32[48]{0:T(128)S(1)}, s32[48]{0:T(128)}, u32[]{:S(2)}) copy-start(s32[48]{0:T(128)} %copy-done.9) | copy-start | bytes 580
  142.9 35.8 %copy-start.12 = (s32[48]{0:T(128)S(1)}, s32[48]{0:T(128)}, u32[]{:S(2)}) copy-start(s32[48]{0:T(128)} %copy-done.11) | copy-start | bytes 580
  172.1 7.0 %copy-start.1 = (bf16[128,1,2,2048]{3,2,1,0:T(2,128)(2,1)}, bf16[128,1,2,2048]{3,2,1,0:T(2,128)(2,1)S(1)}, u32[]{:S(2)}) copy-start(bf16[128,1,2,2048]{3,2,1,0:T(2,128)(2,1)S(1)} %all-to-all-done.4) | copy-start | bytes 3145732
  172.1 41.0 %all-to-all-start.1 = ((bf16[128,1,2,2048]{3,2,1,0:T(2,128)(2,1)}), bf16[128,1,2,2048]{3,2,1,0:T(2,128)(2,1)}, u32[]{:S(2)}, u32[]{:S(2)}) async-start(bf16[128,1,2,2048]{3,2,1,0:T(2,128)(2,1)} %bitcast.85), calls=%async_computation.1 | async-start | bytes 2097152 | tf_op jit(solution)/shard_map/all_to_all | solution.py:87
  216.5 5.1 %copy-start.2 = (f32[8,6,2048]{2,1,0:T(8,128)S(1)}, f32[8,6,2048]{2,1,0:T(8,128)}, u32[]{:S(2)}) copy-start(f32[8,6,2048]{2,1,0:T(8,128)} %reshape.323) | copy-start | bytes 1179652
where the time goes:
time: 226 us; the launch traced here: 225 us
  waiting for transfers between devices  121 us (54%)
  starting transfers between devices  54.1 us (24%)
  local copies, waits for them, and re-layouts  31.8 us (14%)
  other arithmetic  9.01 us (4%)
  matrix products  8.38 us (4%)
    all_to_all x2, waiting for transfers between devices, combine_routes(): lax.all_to_all(partial_value, 'expert', split_axis=0, concat_axis=0, tile...  51.2 us
    all_to_all x1, waiting for transfers between devices, on_device(): lax.all_to_all(outgoing, 'expert', split_axis=0, concat_axis=0, tiled=True)  27.7 us
    all_to_all x1, starting transfers between devices, on_device(): lax.all_to_all(pair_outgoing, 'expert', split_axis=0, concat_axis=0, tile...  20.8 us
    ppermute x2, waiting for transfers between devices, shifted(): return lax.ppermute(block, axis, route)  15.4 us
    all_to_all x1, waiting for transfers between devices, on_device(): lax.all_to_all(grad_outgoing, 'expert', split_axis=0, concat_axis=0, tile...  15.1 us
    all_to_all x2, starting transfers between devices, combine_routes(): lax.all_to_all(partial_value, 'expert', split_axis=0, concat_axis=0, tile...  11.9 us
    all_to_all x1, waiting for transfers between devices, on_device(): lax.all_to_all(pair_outgoing, 'expert', split_axis=0, concat_axis=0, tile...  11.1 us
    all_to_all x1, starting transfers between devices, on_device(): lax.all_to_all(grad_outgoing, 'expert', split_axis=0, concat_axis=0, tile...  7.53 us
  transfers between devices with their start and end apart: 7, of which 7 were waited for; matrix products, arithmetic and copies ran while one was open for 14% of the time, Pallas kernels for 0%

commit v1 on v0

v1 whole, which is shorter than its diff:
```python
import functools

import jax
import jax.numpy as jnp
from jax import lax
from jax.experimental import pallas as pl
from jax.experimental.pallas import tpu as pltpu
from jax.sharding import PartitionSpec as P

CAP = 2
PARTS = 4
LANES = 128
MESH = pl.DeviceIdType.MESH
F32 = jnp.float32
BF16 = jnp.bfloat16


def on_chip(
    groups, sections,
    fwd_ref, froute_ref, fgate_ref, bwd_ref, broute_ref, bgate_ref, saved_ref, wgu_ref, wd_ref,
    out_f, out_b,
    stage, landed, snd, rcv, wide, rows_f, rows_b, rows_p, pairs, part_f, part_b,
    sib_f, sib_b, pass_f, pass_b, near_f, near_b, home_snd, home_rcv,
    shift_s, shift_r, a2a_s, a2a_r, quad_s, quad_r, pair_s, pair_r, red_s, red_r,
):
    seg = lax.axis_index("segment")
    idx = lax.axis_index("expert")
    e = idx // PARTS
    q = idx % PARTS
    xl = q // 2
    c = q % 2
    sib_q = xl * 2 + (1 - c)
    near_q = (1 - xl) * 2 + c
    sib = (seg, e * PARTS + sib_q)
    near = (seg, e * PARTS + near_q)
    slots = CAP * groups
    width = wd_ref.shape[1]
    part = wd_ref.shape[0]
    tokens, top = froute_ref.shape
    blocks = width // LANES
    chunk = CAP * blocks

    def remote(src, dst, ss, rs, where):
        return pltpu.make_async_remote_copy(
            src_ref=src, dst_ref=dst, send_sem=ss, recv_sem=rs, device_id=where, device_id_type=MESH
        )

    half = width // 2
    for i, ref in enumerate((fwd_ref, bwd_ref)):
        v = ref[...].astype(F32)
        stage[i] = jnp.concatenate([v[:, :half], v[:, half:]], axis=0).astype(BF16)

    barrier = pltpu.get_barrier_semaphore()

    @pl.loop(1, groups)
    def _(i):
        pl.semaphore_signal(barrier, inc=1, device_id=(seg, (e + i) % groups * PARTS + q), device_id_type=MESH)

    for i in range(1, PARTS):
        pl.semaphore_signal(barrier, inc=1, device_id=(seg, e * PARTS + (q + i) % PARTS), device_id_type=MESH)
    after = (seg + 1) % sections
    before = (seg + sections - 1) % sections
    for there in (after, before):
        pl.semaphore_signal(barrier, inc=1, device_id=(there, idx), device_id_type=MESH)
    pl.semaphore_wait(barrier, groups + PARTS)

    shifts = [
        remote(stage.at[i], landed.at[i], shift_s.at[i], shift_r.at[i], (there, idx))
        for i, there in enumerate((after, before))
    ]
    for s in shifts:
        s.start()

    lane = lax.broadcasted_iota(jnp.int32, (tokens, slots), 1)
    lane_e = lane // CAP
    lane_c = (lane % CAP).astype(F32)
    earlier = (
        lax.broadcasted_iota(jnp.int32, (tokens, tokens), 1) < lax.broadcasted_iota(jnp.int32, (tokens, tokens), 0)
    ).astype(F32)

    def matches(route_ref, gate_ref):
        hits = [(route_ref[:, k:k + 1] == lane_e).astype(F32) for k in range(top)]
        named = functools.reduce(jnp.add, hits)
        rank = jnp.dot(earlier, named, preferred_element_type=F32)
        sel = jnp.where(rank == lane_c, named, 0.0)
        weight = functools.reduce(jnp.add, [hits[k] * gate_ref[:, k:k + 1] for k in range(top)]) * sel
        return hits, sel, weight

    fhits, fsel, fweight = matches(froute_ref, fgate_ref)
    bhits, bsel, bweight = matches(broute_ref, bgate_ref)
    psel = jnp.concatenate([h * bsel for h in bhits], axis=0)

    def pick(sel, rows):
        return lax.dot_general(
            sel.T.astype(BF16), rows, (((1,), (0,)), ((), ())), preferred_element_type=F32
        )

    def to_chunks(values, out):
        for b in range(blocks):
            wide[pl.ds(b, slots, stride=blocks), :] = values[:, b * LANES:(b + 1) * LANES]
        out[...] = wide[...].astype(BF16)

    def to_rows(ref):
        wide[...] = ref[...].astype(F32)
        return jnp.concatenate([wide[pl.ds(b, slots, stride=blocks), :] for b in range(blocks)], axis=1)

    def exchange(send, recv, ss, rs):
        own = pl.ds(pl.multiple_of(e * chunk, chunk), chunk)

        @pl.loop(1, groups)
        def _(i):
            there = (e + i) % groups
            remote(
                send.at[pl.ds(pl.multiple_of(there * chunk, chunk), chunk)], recv.at[own], ss, rs,
                (seg, there * PARTS + q),
            ).start()

        recv[own, :] = send[own, :]

    def all_of(send, recv, ss, rs):
        n = (groups - 1) * chunk
        return remote(send.at[pl.ds(0, n)], recv.at[pl.ds(0, n)], ss, rs, sib)

    ROWS = lambda k: pl.ds(pl.multiple_of(k * slots, slots), slots)

    to_chunks(pick(psel, saved_ref[...]), snd.at[2])
    exchange(snd.at[2], rcv.at[2], a2a_s.at[2], a2a_r.at[2])

    def unstaged(i):
        shifts[i].wait_recv()
        v = landed[i].astype(F32)
        return jnp.concatenate([v[:tokens], v[tokens:]], axis=1)

    arrived = unstaged(0)
    to_chunks(pick(fsel, arrived.astype(BF16)), snd.at[0])
    exchange(snd.at[0], rcv.at[0], a2a_s.at[0], a2a_r.at[0])
    returning = unstaged(1)
    to_chunks(pick(bsel, returning.astype(BF16)), snd.at[1])
    exchange(snd.at[1], rcv.at[1], a2a_s.at[1], a2a_r.at[1])

    def share_out(d, rows):
        all_of(snd.at[d], rcv.at[d], a2a_s.at[d], a2a_r.at[d]).wait_recv()
        rows[ROWS(q), :] = to_rows(rcv.at[d]).astype(BF16)
        to_near = remote(rows.at[ROWS(q)], rows.at[ROWS(q)], quad_s.at[d, 0], quad_r.at[d, 0], near)
        to_sib = remote(rows.at[ROWS(q)], rows.at[ROWS(q)], quad_s.at[d, 1], quad_r.at[d, 1], sib)
        to_near.start()
        to_sib.start()
        return to_near, to_sib

    def hand_on(d, rows, to_near):
        to_near.wait_recv()
        on = remote(rows.at[ROWS(near_q)], rows.at[ROWS(near_q)], quad_s.at[d, 2], quad_r.at[d, 2], sib)
        on.start()
        return on

    f_near, f_sib = share_out(0, rows_f)

    all_of(snd.at[2], rcv.at[2], a2a_s.at[2], a2a_r.at[2]).wait_recv()
    rows_p[...] = to_rows(rcv.at[2]).astype(BF16)
    pair_copies = []
    for i in range(1, PARTS):
        there = (q + i) % PARTS
        for g in range(2):
            pair_copies.append(
                remote(
                    rows_p.at[:, pl.ds(pl.multiple_of((g * PARTS + there) * part, part), part)],
                    pairs.at[ROWS(q), pl.ds(g * part, part)],
                    pair_s.at[i - 1, g], pair_r.at[i - 1, g], (seg, e * PARTS + there),
                )
            )
            pair_copies[-1].start()
    for g in range(2):
        pairs[ROWS(q), pl.ds(g * part, part)] = rows_p[
            :, pl.ds(pl.multiple_of((g * PARTS + q) * part, part), part)
        ]

    f_on = hand_on(0, rows_f, f_near)
    b_near, b_sib = share_out(1, rows_b)

    f_sib.wait_recv()
    f_on.wait_recv()
    both = jnp.dot(rows_f[...], wgu_ref[...], preferred_element_type=F32)
    gate = both[:, :part]
    hidden = (gate / (1.0 + jnp.exp(-gate)) * both[:, part:]).astype(BF16)
    part_f[...] = jnp.dot(hidden, wd_ref[...], preferred_element_type=F32).astype(BF16)

    def sum_sib(d, parts, from_sib):
        copies = []
        for x in range(2):
            copies.append(
                remote(parts.at[ROWS(x * 2 + 1 - c)], from_sib.at[x], red_s.at[d, x], red_r.at[d, x], sib)
            )
            copies[-1].start()
        return copies

    f_red = sum_sib(0, part_f, sib_f)
    b_on = hand_on(1, rows_b, b_near)

    def sum_near(d, parts, from_sib, passed, from_near, copies):
        for one in copies:
            one.wait_recv()
        passed[...] = (parts[ROWS(near_q), :].astype(F32) + from_sib[1 - xl].astype(F32)).astype(BF16)
        one = remote(passed, from_near, red_s.at[d, 2], red_r.at[d, 2], near)
        one.start()
        return one

    f_pass = sum_near(0, part_f, sib_f, pass_f, near_f, f_red)

    b_sib.wait_recv()
    b_on.wait_recv()
    for one in pair_copies:
        one.wait_recv()
    grad_hidden = lax.dot_general(rows_b[...], wd_ref[...], (((1,), (1,)), ((), ())), preferred_element_type=F32)
    a = pairs[:, :part].astype(F32)
    b = pairs[:, part:].astype(F32)
    sig = 1.0 / (1.0 + jnp.exp(-a))
    grad_gate = (grad_hidden * b * sig * (1.0 + a * (1.0 - sig))).astype(BF16)
    grad_upper = (grad_hidden * (a * sig)).astype(BF16)
    both_grads = jnp.concatenate([grad_gate, grad_upper], axis=1)
    part_b[...] = lax.dot_general(
        both_grads, wgu_ref[...], (((1,), (1,)), ((), ())), preferred_element_type=F32
    ).astype(BF16)
    b_red = sum_sib(1, part_b, sib_b)

    def go_home(d, parts, from_sib, from_near, copy):
        copy.wait_recv()
        total = parts[ROWS(q), :].astype(F32) + from_sib[xl].astype(F32) + from_near[...].astype(F32)
        to_chunks(total, home_snd.at[d])
        exchange(home_snd.at[d], home_rcv.at[d], a2a_s.at[3 + d], a2a_r.at[3 + d])

    go_home(0, part_f, sib_f, near_f, f_pass)
    b_pass = sum_near(1, part_b, sib_b, pass_b, near_b, b_red)
    go_home(1, part_b, sib_b, near_b, b_pass)

    def finish(d, weight, residual, out):
        all_of(home_snd.at[d], home_rcv.at[d], a2a_s.at[3 + d], a2a_r.at[3 + d]).wait_recv()
        rows = to_rows(home_rcv.at[d]).astype(BF16)
        high = weight.astype(BF16)
        low = (weight - high.astype(F32)).astype(BF16)
        mixed = jnp.dot(high, rows, preferred_element_type=F32) + jnp.dot(low, rows, preferred_element_type=F32)
        out[...] = (residual + mixed).astype(BF16)

    finish(0, fweight, arrived, out_f)
    finish(1, bweight, returning, out_b)

    for s in (*shifts, f_near, f_sib, f_on, b_near, b_sib, b_on, *pair_copies, *f_red, *b_red, f_pass, b_pass):
        s.wait_send()
    for d in range(3):
        all_of(snd.at[d], rcv.at[d], a2a_s.at[d], a2a_r.at[d]).wait_send()
    for d in range(2):
        all_of(home_snd.at[d], home_rcv.at[d], a2a_s.at[3 + d], a2a_r.at[3 + d]).wait_send()


def on_device(
    groups, sections,
    forward_input, forward_routes, forward_gates, backward_grad, backward_routes, backward_gates,
    saved_gate_up, w_gate_up, w_down,
):
    _, tokens, width = forward_input.shape
    top = forward_routes.shape[-1]
    hidden = saved_gate_up.shape[-1]
    part = w_down.shape[1]
    slots = CAP * groups
    saved = jnp.transpose(saved_gate_up[0], (1, 0, 2, 3)).reshape(top * tokens, 2 * hidden)
    wgu = w_gate_up[0].reshape(width, 2 * part)
    vmem = pl.BlockSpec(memory_space=pltpu.VMEM)
    long = slots * width // LANES
    row = jax.ShapeDtypeStruct((tokens, width), BF16)
    dma = pltpu.SemaphoreType.DMA
    out_f, out_b = pl.pallas_call(
        functools.partial(on_chip, groups, sections),
        out_shape=(row, row),
        in_specs=[vmem] * 9,
        out_specs=(vmem, vmem),
        scratch_shapes=[
            pltpu.VMEM((2, 2 * tokens, width // 2), BF16),
            pltpu.VMEM((2, 2 * tokens, width // 2), BF16),
            pltpu.VMEM((3, long, LANES), BF16),
            pltpu.VMEM((3, long, LANES), BF16),
            pltpu.VMEM((long, LANES), F32),
            pltpu.VMEM((PARTS * slots, width), BF16),
            pltpu.VMEM((PARTS * slots, width), BF16),
            pltpu.VMEM((slots, 2 * hidden), BF16),
            pltpu.VMEM((PARTS * slots, 2 * part), BF16),
            pltpu.VMEM((PARTS * slots, width), BF16),
            pltpu.VMEM((PARTS * slots, width), BF16),
            pltpu.VMEM((2, slots, width), BF16),
            pltpu.VMEM((2, slots, width), BF16),
            pltpu.VMEM((slots, width), BF16),
            pltpu.VMEM((slots, width), BF16),
            pltpu.VMEM((slots, width), BF16),
            pltpu.VMEM((slots, width), BF16),
            pltpu.VMEM((2, long, LANES), BF16),
            pltpu.VMEM((2, long, LANES), BF16),
            dma((2,)), dma((2,)), dma((5,)), dma((5,)), dma((2, 3)), dma((2, 3)),
            dma((PARTS - 1, 2)), dma((PARTS - 1, 2)), dma((2, 3)), dma((2, 3)),
        ],
        compiler_params=pltpu.CompilerParams(
            collective_id=0, has_side_effects=True, vmem_limit_bytes=40 * 2**20
        ),
    )(
        forward_input[0], forward_routes[0], forward_gates[0], backward_grad[0], backward_routes[0],
        backward_gates[0], saved, wgu, w_down[0],
    )
    return out_f[None], out_b[None]


def solution(mesh):
    spec = P("segment", "expert", None)
    placed = (
        spec, spec, spec, spec, spec, spec,
        P("segment", "expert", None, None, None),
        P("segment", None, None, "expert"),
        spec,
    )
    return jax.shard_map(
        functools.partial(on_device, mesh.shape["expert"] // PARTS, mesh.shape["segment"]),
        mesh=mesh,
        in_specs=placed,
        out_specs=(spec, spec),
        check_vma=False,
    )
```

time: 226 us -> 90.7 us (0.40)
  waiting for transfers between devices: 121 us -> 0 us
  Pallas kernels: 0 us -> 81.4 us
  starting transfers between devices: 54.1 us -> 0 us
  local copies, waits for them, and re-layouts: 31.8 us -> 7.39 us
  other arithmetic: 9.01 us -> 0 us
  matrix products: 8.38 us -> 0 us
    all_to_all x5 -> x0, waiting for transfers between devices: 105 us -> none  [the longest x2 51.2 us: combine_routes(): lax.all_to_all(partial_value, 'expert', split_axis=0, concat_axis=0, tile...]
    pallas_call x0 -> x1, Pallas kernels: none -> 81.4 us  [on_device(): pl.pallas_call(functools.partial(on_chip, groups, sections), out_shape=(r...]
    all_to_all x5 -> x0, starting transfers between devices: 47.3 us -> none  [the longest x1 20.8 us: on_device(): lax.all_to_all(pair_outgoing, 'expert', split_axis=0, concat_axis=0, tile...]
    ppermute x2 -> x0, waiting for transfers between devices: 15.4 us -> none  [shifted(): return lax.ppermute(block, axis, route)]
    another operation x8 -> x0, local copies, waits for them, and re-layouts: 9.82 us -> none
    dot_general x7 -> x0, matrix products: 8.38 us -> none  [the longest x1 2.02 us: expert_backward(): jnp.einsum('erd,efd->erf', flat_grads, down_parts, preferred_element_type...]
    reshape x10 -> x0, local copies, waits for them, and re-layouts: 8.12 us -> none  [the longest x2 2.93 us: combine_routes(): flat_back = returned.reshape(-1, row_width)]
    ppermute x2 -> x0, starting transfers between devices: 6.84 us -> none  [shifted(): return lax.ppermute(block, axis, route)]
  transfers between devices with their start and end apart: 7 -> 0, of which waited for: 7 -> 0; matrix products, arithmetic and copies ran while one was open for 14% -> 0% of each run, Pallas kernels for 0% -> 0%
where the time goes in v1:
time: 90.7 us; the launch traced here: 89.5 us
  Pallas kernels  81.4 us (90%)
  local copies, waits for them, and re-layouts  7.39 us (8%)
    pallas_call x1, Pallas kernels, on_device(): pl.pallas_call(functools.partial(on_chip, groups, sections), out_shape=(r...  81.4 us
    unnamed x13, local copies, waits for them, and re-layouts  6.4 us

profile of v1, /device:TPU:1, one launch (start us, length us, event | category | flops | bytes accessed | tf_op | source)
XLA Modules:
  0.0 89.5 jit_solution(1458492291530094283)
XLA Ops:
  0.6 0.8 copy.11
  1.4 0.8 copy.12
  2.1 0.8 copy.13
  2.9 0.8 copy.14
  3.7 1.0 %copy.15 = bf16[6,8,2,1024]{3,1,2,0:T(8,128)(2,1)S(1)} copy(bf16[6,8,2,1024]{3,2,0,1:T(2,128)(2,1)} %bitcast.28) | data formatting | bytes 393216 | tf_op jit(solution)/shard_map/transpose | solution.py:264
  4.7 0.0 copy-start
  4.7 0.0 copy-start.1
  4.7 0.0 copy-start.2
  4.7 2.1 %copy.16 = bf16[256,8,2,256]{3,1,2,0:T(8,128)(2,1)S(1)} copy(bf16[256,8,2,256]{3,2,1,0:T(2,128)(2,1)} %bitcast.27) | data formatting | bytes 4194304
  6.8 0.0 copy-done
  6.8 0.0 copy-done.1
  6.8 0.0 copy-done.2
  6.8 81.4 %shard_map.104 = (bf16[8,2048]{1,0:T(8,128)(2,1)S(1)}, bf16[8,2048]{1,0:T(8,128)(2,1)S(1)}) custom-call(bf16[8,2048]{1,0:T(8,128)(2,1)S(1)} %bitcast.21, s32[8,6]{1,0:T(8,128)S(1)} %bitcast.23, f32[8,6]{1,0:T(8,128)S(1)} %bitcast.24, bf16[8,2048]{1,0:T(8,128)(2,1)S(1)} %bitcast.22, s32[8,6]{1,0:T(8,128)S(1)} %bitcast.25, f32[8,6]{1,0:T(8,128)S(1)} %bitcast.26, ...), custom_call_target="tpu_custom_call" | custom-call | tf_op jit(solution)/shard_map/pallas_call | solution.py:270
  88.3 0.6 copy.19
  88.9 0.6 copy.20
Async XLA Ops:
  4.7 2.2 %copy-start = (bf16[1,256,2048]{2,1,0:T(8,128)(2,1)S(1)}, bf16[1,256,2048]{2,1,0:T(8,128)(2,1)}, u32[]{:S(2)}) copy-start(bf16[1,256,2048]{2,1,0:T(8,128)(2,1)} %param.17) | copy-start | bytes 3145732
  4.7 2.2 %copy-start.1 = (bf16[1,8,2048]{2,1,0:T(8,128)(2,1)S(1)}, bf16[1,8,2048]{2,1,0:T(8,128)(2,1)}, u32[]{:S(2)}) copy-start(bf16[1,8,2048]{2,1,0:T(8,128)(2,1)} %param.9) | copy-start | bytes 98308
  4.7 2.2 %copy-start.2 = (bf16[1,8,2048]{2,1,0:T(8,128)(2,1)S(1)}, bf16[1,8,2048]{2,1,0:T(8,128)(2,1)}, u32[]{:S(2)}) copy-start(bf16[1,8,2048]{2,1,0:T(8,128)(2,1)} %param.12) | copy-start | bytes 98308

commit v2 on v1

v2 whole, which is shorter than its diff:
```python
import functools

import jax
import jax.numpy as jnp
from jax import lax
from jax.experimental import pallas as pl
from jax.experimental.pallas import tpu as pltpu
from jax.sharding import PartitionSpec as P

CAP = 2
PARTS = 4
LANES = 128
MESH = pl.DeviceIdType.MESH
F32 = jnp.float32
BF16 = jnp.bfloat16


def on_chip(
    groups, sections,
    fwd_hbm, bwd_hbm, froute_hbm, fgate_hbm, broute_hbm, bgate_hbm, saved_hbm, wgu_hbm, wd_hbm,
    out_f, out_b,
    fwd_ref, bwd_ref, froute_ref, fgate_ref, broute_ref, bgate_ref, saved_ref, wgu_raw, wd_ref,
    stage, landed, wgu_ref, saved_rows, wide,
    snd, rcv, rows, pair_rows, pairs, parts, from_sib, passed, from_near, home_snd, home_rcv,
    load_s, shift_s, shift_r, a2a_s, a2a_r, quad_s, quad_r, pair_s, pair_r, red_s, red_r,
):
    seg = lax.axis_index("segment")
    idx = lax.axis_index("expert")
    e = idx // PARTS
    q = idx % PARTS
    xl = q // 2
    c = q % 2
    near_q = (1 - xl) * 2 + c
    sib = (seg, e * PARTS + xl * 2 + (1 - c))
    near = (seg, e * PARTS + near_q)
    width = wd_ref.shape[1]
    part = wd_ref.shape[0]
    top, _, tokens = froute_ref.shape
    blocks = width // LANES
    half = width // 2
    sent = []

    def remote(src, dst, ss, rs, where):
        return pltpu.make_async_remote_copy(
            src_ref=src, dst_ref=dst, send_sem=ss, recv_sem=rs, device_id=where, device_id_type=MESH
        )

    def send(*what):
        copy = remote(*what)
        copy.start()
        sent.append(copy)
        return copy

    def peer(there):
        return (seg, there * PARTS + (q + 2 * ((e + there) % 2)) % PARTS)

    loads = [
        pltpu.make_async_copy(there, here, load_s.at[i])
        for i, (there, here) in enumerate((
            (fwd_hbm, fwd_ref), (bwd_hbm, bwd_ref), (froute_hbm, froute_ref), (fgate_hbm, fgate_ref),
            (broute_hbm, broute_ref), (bgate_hbm, bgate_ref), (saved_hbm, saved_ref), (wgu_hbm, wgu_raw),
            (wd_hbm, wd_ref),
        ))
    ]
    for one in loads:
        one.start()

    barrier = pltpu.get_barrier_semaphore()

    @pl.loop(1, groups)
    def _(i):
        pl.semaphore_signal(barrier, inc=1, device_id=peer((e + i) % groups), device_id_type=MESH)

    for i in range(1, PARTS):
        pl.semaphore_signal(barrier, inc=1, device_id=(seg, e * PARTS + (q + i) % PARTS), device_id_type=MESH)
    after = (seg + 1) % sections
    before = (seg + sections - 1) % sections
    for there in (after, before):
        pl.semaphore_signal(barrier, inc=1, device_id=(there, idx), device_id_type=MESH)

    for i, ref in enumerate((fwd_ref, bwd_ref)):
        loads[i].wait()
        v = ref[...].astype(F32)
        stage[i] = jnp.concatenate([v[:, :half], v[:, half:]], axis=0).astype(BF16)

    pl.semaphore_wait(barrier, groups + PARTS)
    shifts = [
        send(stage.at[i], landed.at[i], shift_s.at[i], shift_r.at[i], (there, idx))
        for i, there in enumerate((after, before))
    ]

    for one in loads[2:7]:
        one.wait()
    for g in range(2):
        saved_rows[:, g * half:(g + 1) * half] = saved_ref[:, g, :]

    row_e = lax.broadcasted_iota(jnp.int32, (groups, tokens), 0)
    prior = (
        lax.broadcasted_iota(jnp.int32, (tokens, tokens), 0) < lax.broadcasted_iota(jnp.int32, (tokens, tokens), 1)
    ).astype(F32)

    def matches(route_ref, gate_ref):
        hits = [(row_e == route_ref[k]).astype(F32) for k in range(top)]
        named = functools.reduce(jnp.add, hits)
        rank = jnp.dot(named, prior, preferred_element_type=F32)
        gate = functools.reduce(jnp.add, [hits[k] * gate_ref[k] for k in range(top)])
        sels = [jnp.where(rank == float(h), named, 0.0) for h in range(CAP)]
        return hits, sels, [(gate * s).T for s in sels]

    bhits, bsels, bweights = matches(broute_ref, bgate_ref)
    fhits, fsels, fweights = matches(froute_ref, fgate_ref)
    n = top * tokens
    kt = lax.broadcasted_iota(jnp.int32, (n, n), 0)
    tk = lax.broadcasted_iota(jnp.int32, (n, n), 1)
    turn = ((kt % tokens) * top + kt // tokens == tk).astype(F32)
    psels = [
        jnp.dot(jnp.concatenate([h * s for h in bhits], axis=1), turn, preferred_element_type=F32) for s in bsels
    ]

    def pick(sel, values):
        return jnp.dot(sel.astype(BF16), values, preferred_element_type=F32)

    def to_chunks(values, out):
        for b in range(blocks):
            wide[pl.ds(b, groups, stride=blocks), :] = values[:, b * LANES:(b + 1) * LANES]
        out[...] = wide[...].astype(BF16)

    def to_rows(ref):
        wide[...] = ref[...].astype(F32)
        return jnp.concatenate(
            [wide[pl.ds(b, groups, stride=blocks), :].astype(BF16) for b in range(blocks)], axis=1
        )

    span = (groups - 1) * blocks

    def exchange(src, dst, s):
        own = pl.ds(pl.multiple_of(e * blocks, blocks), blocks)

        @pl.loop(1, groups)
        def _(i):
            there = (e + i) % groups
            remote(
                src.at[pl.ds(pl.multiple_of(there * blocks, blocks), blocks)], dst.at[own],
                a2a_s.at[s], a2a_r.at[s], peer(there),
            ).start()

        dst[own, :] = src[own, :]
        whole = remote(src.at[pl.ds(0, span)], dst.at[pl.ds(0, span)], a2a_s.at[s], a2a_r.at[s], sib)
        sent.append(whole)
        return whole

    def ROWS(k):
        return pl.ds(pl.multiple_of(k * groups, groups), groups)

    came, shares, ons, sibs, passes, homes, pair_copies = {}, {}, {}, {}, {}, {}, {}

    def dispatch(u, sel, values):
        to_chunks(pick(sel, values), snd.at[u])
        came[u] = exchange(snd.at[u], rcv.at[u], u)

    def share_out(u):
        came[u].wait_recv()
        mine = rows.at[u, ROWS(q)]
        mine[...] = to_rows(rcv.at[u])
        shares[u] = (
            send(mine, mine, quad_s.at[u, 0], quad_r.at[u, 0], near),
            send(mine, mine, quad_s.at[u, 1], quad_r.at[u, 1], sib),
        )

    def hand_on(u):
        shares[u][0].wait_recv()
        other = rows.at[u, ROWS(near_q)]
        ons[u] = send(other, other, quad_s.at[u, 2], quad_r.at[u, 2], sib)

    def share_pairs(h):
        came[4 + h].wait_recv()
        pair_rows[h] = to_rows(rcv.at[4 + h])
        cols = [
            [pl.ds(pl.multiple_of((g * PARTS + (q + i) % PARTS) * part, part), part) for g in range(2)]
            for i in range(PARTS)
        ]
        pair_copies[h] = [
            send(
                pair_rows.at[h, :, cols[i][g]], pairs.at[h, ROWS(q), pl.ds(g * part, part)],
                pair_s.at[h, i - 1, g], pair_r.at[h, i - 1, g], (seg, e * PARTS + (q + i) % PARTS),
            )
            for i in range(1, PARTS)
            for g in range(2)
        ]
        for g in range(2):
            pairs[h, ROWS(q), g * part:(g + 1) * part] = pair_rows[h, :, cols[0][g]]

    def compute(u):
        shares[u][1].wait_recv()
        ons[u].wait_recv()
        if u < CAP:
            both = jnp.dot(rows[u], wgu_ref[...], preferred_element_type=F32)
            gate = both[:, :part]
            hidden = (gate / (1.0 + jnp.exp(-gate)) * both[:, part:]).astype(BF16)
            parts[u] = jnp.dot(hidden, wd_ref[...], preferred_element_type=F32).astype(BF16)
        else:
            h = u - CAP
            for one in pair_copies[h]:
                one.wait_recv()
            grad_hidden = lax.dot_general(
                rows[u], wd_ref[...], (((1,), (1,)), ((), ())), preferred_element_type=F32
            )
            a = pairs[h, :, :part].astype(F32)
            b = pairs[h, :, part:].astype(F32)
            sig = 1.0 / (1.0 + jnp.exp(-a))
            grad_gate = (grad_hidden * b * sig * (1.0 + a * (1.0 - sig))).astype(BF16)
            grad_upper = (grad_hidden * (a * sig)).astype(BF16)
            parts[u] = lax.dot_general(
                jnp.concatenate([grad_gate, grad_upper], axis=1), wgu_ref[...],
                (((1,), (1,)), ((), ())), preferred_element_type=F32,
            ).astype(BF16)
        sibs[u] = [
            send(parts.at[u, ROWS(x * 2 + 1 - c)], from_sib.at[u, x], red_s.at[u, x], red_r.at[u, x], sib)
            for x in range(2)
        ]

    def sum_core(u):
        for one in sibs[u]:
            one.wait_recv()
        passed[u] = (parts[u, ROWS(near_q), :].astype(F32) + from_sib[u, 1 - xl].astype(F32)).astype(BF16)
        passes[u] = send(passed.at[u], from_near.at[u], red_s.at[u, 2], red_r.at[u, 2], near)

    def go_home(u):
        passes[u].wait_recv()
        total = parts[u, ROWS(q), :].astype(F32) + from_sib[u, xl].astype(F32) + from_near[u].astype(F32)
        to_chunks(total, home_snd.at[u])
        homes[u] = exchange(home_snd.at[u], home_rcv.at[u], 6 + u)

    def combined(u, weight):
        homes[u].wait_recv()
        back = to_rows(home_rcv.at[u])
        high = weight.astype(BF16)
        low = (weight - high.astype(F32)).astype(BF16)
        return jnp.dot(high, back, preferred_element_type=F32) + jnp.dot(low, back, preferred_element_type=F32)

    def unstaged(i):
        shifts[i].wait_recv()
        v = landed[i].astype(F32)
        return jnp.concatenate([v[:tokens], v[tokens:]], axis=1)

    steps = 8
    step = width // steps

    def lay_out(first, last):
        @pl.loop(first, last)
        def _(i):
            some = pl.ds(pl.multiple_of(i * step, step), step)
            for g in range(2):
                wgu_ref[some, g * part:(g + 1) * part] = wgu_raw[some, g, :]

    arrived = unstaged(0)
    dispatch(0, fsels[0], arrived.astype(BF16))
    dispatch(4, psels[0], saved_rows[...])
    dispatch(1, fsels[1], arrived.astype(BF16))
    returning = unstaged(1)
    dispatch(2, bsels[0], returning.astype(BF16))
    for one in loads[7:]:
        one.wait()
    lay_out(0, steps)
    share_out(0)
    share_pairs(0)
    dispatch(5, psels[1], saved_rows[...])
    dispatch(3, bsels[1], returning.astype(BF16))
    share_out(1)
    hand_on(0)
    share_out(2)
    compute(0)
    hand_on(1)
    sum_core(0)
    share_pairs(1)
    compute(1)
    hand_on(2)
    sum_core(1)
    share_out(3)
    compute(2)
    go_home(0)
    sum_core(2)
    go_home(1)
    hand_on(3)
    compute(3)
    go_home(2)
    sum_core(3)
    mixed_f = combined(0, fweights[0])
    go_home(3)
    out_f[...] = (arrived + mixed_f + combined(1, fweights[1])).astype(BF16)
    mixed_b = combined(2, bweights[0])
    out_b[...] = (returning + mixed_b + combined(3, bweights[1])).astype(BF16)

    for one in sent:
        one.wait_send()


def on_device(
    groups, sections,
    forward_input, forward_routes, forward_gates, backward_grad, backward_routes, backward_gates,
    saved_gate_up, w_gate_up, w_down,
):
    _, tokens, width = forward_input.shape
    top = forward_routes.shape[-1]
    hidden = saved_gate_up.shape[-1]
    part = w_down.shape[1]
    hbm = pl.BlockSpec(memory_space=pl.ANY)
    long = groups * width // LANES
    row = jax.ShapeDtypeStruct((tokens, width), BF16)
    dma = pltpu.SemaphoreType.DMA
    units = 2 * CAP
    by_top = lambda v: jnp.transpose(v, (2, 0, 1))
    out_f, out_b = pl.pallas_call(
        functools.partial(on_chip, groups, sections),
        out_shape=(row, row),
        in_specs=[hbm] * 9,
        out_specs=(pl.BlockSpec(memory_space=pltpu.VMEM),) * 2,
        scratch_shapes=[
            pltpu.VMEM((tokens, width), BF16),
            pltpu.VMEM((tokens, width), BF16),
            pltpu.VMEM((top, 1, tokens), jnp.int32),
            pltpu.VMEM((top, 1, tokens), F32),
            pltpu.VMEM((top, 1, tokens), jnp.int32),
            pltpu.VMEM((top, 1, tokens), F32),
            pltpu.VMEM((tokens * top, 2, hidden), BF16),
            pltpu.VMEM((width, 2, part), BF16),
            pltpu.VMEM((part, width), BF16),
            pltpu.VMEM((2, 2 * tokens, width // 2), BF16),
            pltpu.VMEM((2, 2 * tokens, width // 2), BF16),
            pltpu.VMEM((width, 2 * part), BF16),
            pltpu.VMEM((tokens * top, 2 * hidden), BF16),
            pltpu.VMEM((long, LANES), F32),
            pltpu.VMEM((units + CAP, long, LANES), BF16),
            pltpu.VMEM((units + CAP, long, LANES), BF16),
            pltpu.VMEM((units, PARTS * groups, width), BF16),
            pltpu.VMEM((CAP, groups, 2 * hidden), BF16),
            pltpu.VMEM((CAP, PARTS * groups, 2 * part), BF16),
            pltpu.VMEM((units, PARTS * groups, width), BF16),
            pltpu.VMEM((units, 2, groups, width), BF16),
            pltpu.VMEM((units, groups, width), BF16),
            pltpu.VMEM((units, groups, width), BF16),
            pltpu.VMEM((units, long, LANES), BF16),
            pltpu.VMEM((units, long, LANES), BF16),
            dma((9,)), dma((2,)), dma((2,)),
            dma((2 * units + CAP,)), dma((2 * units + CAP,)), dma((units, 3)), dma((units, 3)),
            dma((CAP, PARTS - 1, 2)), dma((CAP, PARTS - 1, 2)), dma((units, 3)), dma((units, 3)),
        ],
        compiler_params=pltpu.CompilerParams(
            collective_id=0, has_side_effects=True, vmem_limit_bytes=62 * 2**20
        ),
    )(
        forward_input[0], backward_grad[0], by_top(forward_routes), by_top(forward_gates),
        by_top(backward_routes), by_top(backward_gates),
        saved_gate_up[0].reshape(tokens * top, 2, hidden), w_gate_up[0], w_down[0],
    )
    return out_f[None], out_b[None]


def solution(mesh):
    spec = P("segment", "expert", None)
    placed = (
        spec, spec, spec, spec, spec, spec,
        P("segment", "expert", None, None, None),
        P("segment", None, None, "expert"),
        spec,
    )
    return jax.shard_map(
        functools.partial(on_device, mesh.shape["expert"] // PARTS, mesh.shape["segment"]),
        mesh=mesh,
        in_specs=placed,
        out_specs=(spec, spec),
        check_vma=False,
    )
```

time: 90.7 us -> 78.9 us (0.87); the launches traced: 89.5 us -> 78.7 us
  Pallas kernels: 81.4 us -> 75.3 us
  local copies, waits for them, and re-layouts: 7.39 us -> 2.75 us
    pallas_call x1, Pallas kernels: 81.4 us -> 75.3 us  [on_device(): pl.pallas_call(functools.partial(on_chip, groups, sections), out_shape=(r...]
    unnamed x13 -> x2, local copies, waits for them, and re-layouts: 6.4 us -> 2.75 us
    transpose x1 -> x0, local copies, waits for them, and re-layouts: 0.99 us -> none  [on_device(): jnp.transpose(saved_gate_up[0], (1, 0, 2, 3))]
where the time goes in v2:
time: 78.9 us; the launch traced here: 78.7 us
  Pallas kernels  75.3 us (95%)
  local copies, waits for them, and re-layouts  2.75 us (3%)
    pallas_call x1, Pallas kernels, on_device(): pl.pallas_call(functools.partial(on_chip, groups, sections), out_shape=(r...  75.3 us
    unnamed x2, local copies, waits for them, and re-layouts  2.75 us

profile of v2, /device:TPU:1, one launch (start us, length us, event | category | flops | bytes accessed | tf_op | source)
XLA Modules:
  0.0 78.7 jit_solution(6380989939548397911)
XLA Ops:
  0.6 75.3 %shard_map.104 = (bf16[8,2048]{1,0:T(8,128)(2,1)}, bf16[8,2048]{1,0:T(8,128)(2,1)}) custom-call(bf16[8,2048]{1,0:T(8,128)(2,1)} %bitcast.16, bf16[8,2048]{1,0:T(8,128)(2,1)} %bitcast.17, s32[6,1,8]{2,1,0:T(1,128)} %bitcast.18, f32[6,1,8]{2,1,0:T(1,128)} %bitcast.19, s32[6,1,8]{2,1,0:T(1,128)} %bitcast.20, f32[6,1,8]{2,1,0:T(1,128)} %bitcast.21, ...), custom_call_target="tpu_custom_call" | custom-call | tf_op jit(solution)/shard_map/pallas_call | solution.py:313
  75.9 1.4 %copy.13 = bf16[1,8,2048]{2,1,0:T(8,128)(2,1)} copy(bf16[1,8,2048]{2,1,0:T(8,128)(2,1)} %bitcast.15) | data formatting | bytes 65536
  77.3 1.4 %copy.14 = bf16[1,8,2048]{2,1,0:T(8,128)(2,1)} copy(bf16[1,8,2048]{2,1,0:T(8,128)(2,1)} %bitcast.14) | data formatting | bytes 65536

commit v3 on v2

--- a/solution.py
+++ b/solution.py
@@ -18,7 +18,7 @@
 def on_chip(
     groups, sections,
     fwd_hbm, bwd_hbm, froute_hbm, fgate_hbm, broute_hbm, bgate_hbm, saved_hbm, wgu_hbm, wd_hbm,
-    out_f, out_b,
+    out,
     fwd_ref, bwd_ref, froute_ref, fgate_ref, broute_ref, bgate_ref, saved_ref, wgu_raw, wd_ref,
     stage, landed, wgu_ref, saved_rows, wide,
     snd, rcv, rows, pair_rows, pairs, parts, from_sib, passed, from_near, home_snd, home_rcv,
@@ -136,14 +136,24 @@
     def exchange(src, dst, s):
         own = pl.ds(pl.multiple_of(e * blocks, blocks), blocks)
 
-        @pl.loop(1, groups)
-        def _(i):
-            there = (e + i) % groups
+        def to(there):
             remote(
                 src.at[pl.ds(pl.multiple_of(there * blocks, blocks), blocks)], dst.at[own],
                 a2a_s.at[s], a2a_r.at[s], peer(there),
             ).start()
 
+        ring = groups // 4
+        for dz in (1, 0):
+            z = (e // (2 * ring) + dz) % 2
+
+            @pl.loop(0, ring - 1 + dz)
+            def _(j):
+                away = ring // 2 + (j + 1) // 2 * (1 - 2 * (j % 2))
+                y = (e // 2 + away) % ring
+                for dx in (1, 0):
+                    to(z * (2 * ring) + y * 2 + (e + dx) % 2)
+
+        to(e + 1 - 2 * (e % 2))
         dst[own, :] = src[own, :]
         whole = remote(src.at[pl.ds(0, span)], dst.at[pl.ds(0, span)], a2a_s.at[s], a2a_r.at[s], sib)
         sent.append(whole)
@@ -255,41 +265,41 @@
 
     arrived = unstaged(0)
     dispatch(0, fsels[0], arrived.astype(BF16))
-    dispatch(4, psels[0], saved_rows[...])
     dispatch(1, fsels[1], arrived.astype(BF16))
     returning = unstaged(1)
     dispatch(2, bsels[0], returning.astype(BF16))
+    dispatch(4, psels[0], saved_rows[...])
     for one in loads[7:]:
         one.wait()
     lay_out(0, steps)
     share_out(0)
-    share_pairs(0)
-    dispatch(5, psels[1], saved_rows[...])
     dispatch(3, bsels[1], returning.astype(BF16))
     share_out(1)
+    dispatch(5, psels[1], saved_rows[...])
+    share_out(2)
     hand_on(0)
-    share_out(2)
     compute(0)
     hand_on(1)
     sum_core(0)
-    share_pairs(1)
+    share_pairs(0)
     compute(1)
+    share_out(3)
+    sum_core(1)
     hand_on(2)
-    sum_core(1)
-    share_out(3)
     compute(2)
     go_home(0)
+    share_pairs(1)
     sum_core(2)
+    hand_on(3)
     go_home(1)
-    hand_on(3)
     compute(3)
+    sum_core(3)
     go_home(2)
-    sum_core(3)
     mixed_f = combined(0, fweights[0])
     go_home(3)
-    out_f[...] = (arrived + mixed_f + combined(1, fweights[1])).astype(BF16)
+    out[0] = (arrived + mixed_f + combined(1, fweights[1])).astype(BF16)
     mixed_b = combined(2, bweights[0])
-    out_b[...] = (returning + mixed_b + combined(3, bweights[1])).astype(BF16)
+    out[1] = (returning + mixed_b + combined(3, bweights[1])).astype(BF16)
 
     for one in sent:
         one.wait_send()
@@ -310,11 +320,11 @@
     dma = pltpu.SemaphoreType.DMA
     units = 2 * CAP
     by_top = lambda v: jnp.transpose(v, (2, 0, 1))
-    out_f, out_b = pl.pallas_call(
+    out = pl.pallas_call(
         functools.partial(on_chip, groups, sections),
-        out_shape=(row, row),
+        out_shape=jax.ShapeDtypeStruct((2, tokens, width), BF16),
         in_specs=[hbm] * 9,
-        out_specs=(pl.BlockSpec(memory_space=pltpu.VMEM),) * 2,
+        out_specs=pl.BlockSpec(memory_space=pltpu.VMEM),
         scratch_shapes=[
             pltpu.VMEM((tokens, width), BF16),
             pltpu.VMEM((tokens, width), BF16),
@@ -353,7 +363,7 @@
         by_top(backward_routes), by_top(backward_gates),
         saved_gate_up[0].reshape(tokens * top, 2, hidden), w_gate_up[0], w_down[0],
     )
-    return out_f[None], out_b[None]
+    return out[:1], out[1:]
 
 
 def solution(mesh):

time: 78.9 us -> 72.7 us (0.921)
  Pallas kernels: 75.3 us -> 70.5 us
  local copies, waits for them, and re-layouts: 2.75 us -> 1.4 us
    pallas_call x1, Pallas kernels: 75.3 us -> 70.5 us  [on_device(): pl.pallas_call(functools.partial(on_chip, groups, sections), out_shape=ja...]
    unnamed x2 -> x0, local copies, waits for them, and re-layouts: 2.75 us -> none
    slice x0 -> x1, local copies, waits for them, and re-layouts: none -> 1.4 us  [on_device(): return (out[:1], out[1:])]
where the time goes in v3:
time: 72.7 us; the launch traced here: 72.5 us
  Pallas kernels  70.5 us (97%)
  local copies, waits for them, and re-layouts  1.4 us (2%)
    pallas_call x1, Pallas kernels, on_device(): pl.pallas_call(functools.partial(on_chip, groups, sections), out_shape=ja...  70.5 us

profile of v3, /device:TPU:1, one launch (start us, length us, event | category | flops | bytes accessed | tf_op | source)
XLA Modules:
  0.0 72.5 jit_solution(8745687392242214820)
XLA Ops:
  0.6 70.5 %shard_map.104 = bf16[2,8,2048]{2,1,0:T(8,128)(2,1)} custom-call(bf16[8,2048]{1,0:T(8,128)(2,1)} %bitcast.12, bf16[8,2048]{1,0:T(8,128)(2,1)} %bitcast.13, s32[6,1,8]{2,1,0:T(1,128)} %bitcast.14, f32[6,1,8]{2,1,0:T(1,128)} %bitcast.15, s32[6,1,8]{2,1,0:T(1,128)} %bitcast.16, f32[6,1,8]{2,1,0:T(1,128)} %bitcast.17, bf16[48,2,1024]{2,1,0:T(2,128)(2,1)} %bitcast.11, ...), custom_call_target="tpu_custom_call" | custom-call | tf_op jit(solution)/shard_map/pallas_call | solution.py:323
  71.1 1.4 %fusion = (bf16[1,8,2048]{2,1,0:T(8,128)(2,1)}, bf16[1,8,2048]{2,1,0:T(8,128)(2,1)}) fusion(bf16[2,8,2048]{2,1,0:T(8,128)(2,1)} %shard_map.104), kind=kLoop, calls=%fused_computation | loop fusion | bytes 131072 | tf_op jit(solution)/shard_map/slice | solution.py:366

commit v4 on v3

--- a/solution.py
+++ b/solution.py
@@ -288,8 +288,8 @@
     hand_on(2)
     compute(2)
     go_home(0)
+    sum_core(2)
     share_pairs(1)
-    sum_core(2)
     hand_on(3)
     go_home(1)
     compute(3)

time: 72.7 us -> 76 us (1.045)
  Pallas kernels: 70.5 us -> 73.8 us
    pallas_call x1, Pallas kernels: 70.5 us -> 73.8 us  [on_device(): pl.pallas_call(functools.partial(on_chip, groups, sections), out_shape=ja...]
where the time goes in v4:
time: 76 us; the launch traced here: 75.8 us
  Pallas kernels  73.8 us (97%)
  local copies, waits for them, and re-layouts  1.4 us (2%)
    pallas_call x1, Pallas kernels, on_device(): pl.pallas_call(functools.partial(on_chip, groups, sections), out_shape=ja...  73.8 us

profile of v4, /device:TPU:1, one launch (start us, length us, event | category | flops | bytes accessed | tf_op | source)
XLA Modules:
  0.0 75.8 jit_solution(95972933189643199)
XLA Ops:
  0.6 73.8 %shard_map.104 = bf16[2,8,2048]{2,1,0:T(8,128)(2,1)} custom-call(bf16[8,2048]{1,0:T(8,128)(2,1)} %bitcast.12, bf16[8,2048]{1,0:T(8,128)(2,1)} %bitcast.13, s32[6,1,8]{2,1,0:T(1,128)} %bitcast.14, f32[6,1,8]{2,1,0:T(1,128)} %bitcast.15, s32[6,1,8]{2,1,0:T(1,128)} %bitcast.16, f32[6,1,8]{2,1,0:T(1,128)} %bitcast.17, bf16[48,2,1024]{2,1,0:T(2,128)(2,1)} %bitcast.11, ...), custom_call_target="tpu_custom_call" | custom-call | tf_op jit(solution)/shard_map/pallas_call | solution.py:323
  74.4 1.4 %fusion = (bf16[1,8,2048]{2,1,0:T(8,128)(2,1)}, bf16[1,8,2048]{2,1,0:T(8,128)(2,1)}) fusion(bf16[2,8,2048]{2,1,0:T(8,128)(2,1)} %shard_map.104), kind=kLoop, calls=%fused_computation | loop fusion | bytes 131072 | tf_op jit(solution)/shard_map/slice | solution.py:366
